TPU v7x, 256 devices: a whole 4x4x8 slice. The times are simulated.
256 devices in a mesh: dp: 4 (over x), out: 16 (over z, y_lo), in: 4 (over y_hi, core).
Axes of the slice: x: 4, y: 4 (y_hi: 2, y_lo: 2; y = y_hi * 2 + y_lo), z: 8, core: 2. Of those that a mesh axis runs over, the one named last changes fastest.
Arguments:
- activations: bfloat16 [8192, 8192], P(('dp', 'out'), 'in'), may hold values from -0.23925781 to 0.23925781
- out_grad: bfloat16 [8192, 10240], P('dp', 'out'), may hold values from -2.390625 to 2.390625
- weight: bfloat16 [4, 2048, 10240], P('in', 'dp', 'out'), may hold values from -0.0625 to 0.0625
Outputs:
- input_grad: bfloat16 [8192, 8192], P(('dp', 'out'), 'in')
- weight_grad: float32 [4, 2048, 10240], P('in', 'dp', 'out')
All inputs are finite; a program needn't handle non-finite values.
Results may differ from a plain program's by a relative error of at most 0.001.
Values may be sent and summed in bfloat16 or wider, within the bound.
No kernel may reach another device: no remote copies, remote signals or barrier semaphores. Data moves between devices by JAX's collectives and lax.ppermute only.
A program may use at most 128 MiB of HBM per device.

v0:
```python
import jax
import jax.numpy as jnp
from jax import lax
from jax.sharding import PartitionSpec as P


def on_device(activations, out_grad, weight):
    gathered = lax.all_gather(weight, "dp", axis=1, tiled=True)[0]
    grad_rows = out_grad
    summed = lax.psum_scatter(
        lax.dot_general(
            grad_rows, gathered, (((1,), (1,)), ((), ())), preferred_element_type=jnp.float32
        ),
        "out",
        scatter_dimension=0,
        tiled=True,
    )
    input_grad = summed.astype(jnp.bfloat16)
    grad_rows = out_grad
    folded = lax.dot_general(
        lax.all_gather(activations, "out", axis=0, tiled=True),
        grad_rows,
        (((0,), (0,)), ((), ())),
        preferred_element_type=jnp.float32,
    )
    weight_grad = lax.psum_scatter(folded[None], "dp", scatter_dimension=1, tiled=True)
    return (input_grad, weight_grad)


def solution(mesh):
    in_specs = (P(("dp", "out"), "in"), P("dp", "out"), P("in", "dp", "out"))
    out_specs = (P(("dp", "out"), "in"), P("in", "dp", "out"))
    return jax.shard_map(
        on_device, mesh=mesh, in_specs=in_specs, out_specs=out_specs, check_vma=False
    )
```

profile of v0, /device:TPU:4, one launch (start us, length us, event | category | flops | bytes accessed | tf_op | source)
XLA Modules:
  0.0 656.8 jit_solution(14127751710623876923)
XLA Ops:
  7.2 0.0 copy-start
  7.2 0.0 all-gather.3.cloned.1.call-start
  7.2 0.7 all-gather.3.cloned.1.call-update
  7.9 0.0 all-gather.5.cloned.1.call-start
  8.0 0.7 all-gather.5.cloned.1.call-update
  8.7 0.0 reduce-scatter.3.cloned.1.call-start
  8.7 40.6 %all-gather.3.cloned.1.call-done = bf16[1,2048,640]{2,1,0:T(8,128)(2,1)} async-done(((bf16[1,512,640]{2,1,0:T(8,128)(2,1)}), bf16[1,2048,640]{2,1,0:T(8,128)(2,1)}) %all-gather.3.cloned.1.call-update) | async-done | bytes 2621456 | tf_op jit(solution)/shard_map/all_gather | solution.py:8
  49.4 0.0 copy-done
  49.4 11.3 %fusion = f32[2048,2048]{1,0:T(8,128)} fusion(bf16[2048,640]{1,0:T(8,128)(2,1)S(1)} %copy-done, bf16[1,2048,640]{2,1,0:T(8,128)(2,1)} %all-gather.3.cloned.1.call-done), kind=kOutput, calls=%fused_computation.1 | convolution fusion | flops 5368709120 | bytes 22020096 | tf_op jit(solution)/shard_map/dot_general | solution.py:11
  60.7 0.0 reduce-scatter.3.cloned.1.call-update
  60.7 0.0 reduce-scatter.5.cloned.1.call-start
  60.7 174.2 %all-gather.5.cloned.1.call-done = bf16[2048,2048]{1,0:T(8,128)(2,1)} async-done(((bf16[128,2048]{1,0:T(8,128)(2,1)}), bf16[2048,2048]{1,0:T(8,128)(2,1)}) %all-gather.5.cloned.1.call-update) | async-done | bytes 8388624 | tf_op jit(solution)/shard_map/all_gather | solution.py:21
  235.0 10.8 %convolution_bitcast_fusion = f32[1,2048,640]{2,1,0:T(8,128)} fusion(bf16[2048,2048]{1,0:T(8,128)(2,1)} %all-gather.5.cloned.1.call-done, bf16[2048,640]{1,0:T(8,128)(2,1)S(1)} %copy-done), kind=kOutput, calls=%fused_computation | convolution fusion | flops 5368709120 | bytes 16252928 | tf_op jit(solution)/shard_map/dot_general | solution.py:20
  245.7 0.0 reduce-scatter.5.cloned.1.call-update
  245.7 344.2 %reduce-scatter.3.cloned.1.call-done = f32[128,2048]{1,0:T(8,128)} async-done(((f32[2048,2048]{1,0:T(8,128)}), f32[128,2048]{1,0:T(8,128)}) %reduce-scatter.3.cloned.1.call-update) | async-done | bytes 1048592 | tf_op jit(solution)/shard_map/reduce_scatter | solution.py:10
  589.9 2.1 convert_element_type.3
  592.0 58.2 %reduce-scatter.5.cloned.1.call-done = f32[1,512,640]{2,1,0:T(8,128)} async-done(((f32[1,2048,640]{2,1,0:T(8,128)}), f32[1,512,640]{2,1,0:T(8,128)}) %reduce-scatter.5.cloned.1.call-update) | async-done | bytes 1310736 | tf_op jit(solution)/shard_map/reduce_scatter | solution.py:26
Async XLA Ops:
  7.2 42.2 %copy-start = (bf16[2048,640]{1,0:T(8,128)(2,1)S(1)}, bf16[2048,640]{1,0:T(8,128)(2,1)}, u32[]{:S(2)}) copy-start(bf16[2048,640]{1,0:T(8,128)(2,1)} %param.4) | copy-start | bytes 7864324
  7.2 42.2 %all-gather.3.cloned.1.call-start = ((), (), s32[]{:S(2)}) async-start(), calls=%async_computation.2 | async-start | bytes 3276800 | tf_op jit(solution)/shard_map/all_gather | solution.py:8
  7.9 227.0 %all-gather.5.cloned.1.call-start = ((), (), s32[]{:S(2)}) async-start(), calls=%async_computation.4 | async-start | bytes 8912896 | tf_op jit(solution)/shard_map/all_gather | solution.py:21
  8.7 581.3 %reduce-scatter.3.cloned.1.call-start = ((), (), s32[]{:S(2)}) async-start(), calls=%async_computation.3 | async-start | bytes 17825792 | tf_op jit(solution)/shard_map/reduce_scatter | solution.py:10
  60.7 589.6 %reduce-scatter.5.cloned.1.call-start = ((), (), s32[]{:S(2)}) async-start(), calls=%async_computation.5 | async-start | bytes 6553600 | tf_op jit(solution)/shard_map/reduce_scatter | solution.py:26
Sparse Core Ops, SparseCore 0:
  9.8 39.4 all-gather.2
  51.1 183.7 all-gather.4
  237.5 352.3 reduce-scatter.2
  592.9 57.2 reduce-scatter.4
where the time goes:
time: 659 us; the launch traced here: 657 us
  waiting for transfers between devices  619 us (94%)
  matrix products  22.1 us (3%)
  between operations  13.8 us (2%)
    reduce_scatter x1, waiting for transfers between devices, on_device(): lax.psum_scatter(lax.dot_general(grad_rows, gathered, (((1,), (1,)), ((),...  344 us
    all_gather x1, waiting for transfers between devices, on_device(): lax.all_gather(activations, 'out', axis=0, tiled=True)  174 us
    reduce_scatter x1, waiting for transfers between devices, on_device(): lax.psum_scatter(folded[None], 'dp', scatter_dimension=1, tiled=True)  58.2 us
    all_gather x1, waiting for transfers between devices, on_device(): gathered = lax.all_gather(weight, 'dp', axis=1, tiled=True)[0]  40.6 us
  transfers between devices with their start and end apart: 4, of which 4 were waited for; matrix products, arithmetic and copies ran while one was open for 4% of the time, Pallas kernels for 0%

commit v1 on v0

v1 whole, which is shorter than its diff:
```python
import jax
import jax.numpy as jnp
from jax import lax
from jax.sharding import Mesh, PartitionSpec as P

F32 = jnp.float32
BF16 = jnp.bfloat16


def pair_order(first, mine, other):
    return jnp.stack([jnp.where(first, mine, other), jnp.where(first, other, mine)])


def swap(a, axis):
    return lax.ppermute(a, axis, [(0, 1), (1, 0)])


def y_ring(a):
    perm = []
    for y in range(4):
        for c in range(2):
            t = (y + (1 if c == 0 else -1)) % 4
            perm.append((((y % 2) * 2 + y // 2) * 2 + c, ((t % 2) * 2 + t // 2) * 2 + c))
    return lax.ppermute(a, ("yl", "yh", "c"), perm)


def dot(a, b, dims):
    return lax.dot_general(a, b, (dims, ((), ())), preferred_element_type=F32)


def on_device(activations, out_grad, weight):
    h = lax.axis_index("yl")
    c = lax.axis_index("c")
    tokens, width = out_grad.shape
    own_tokens, features = activations.shape
    rows = weight.shape[1]
    half = rows // 2
    owners = features // rows

    acts = activations.reshape(own_tokens, owners, 2, half)
    acts_mine = lax.dynamic_index_in_dim(acts, h, 2, keepdims=False).reshape(own_tokens, -1)
    acts_sent = lax.dynamic_index_in_dim(acts, 1 - h, 2, keepdims=False).reshape(own_tokens, -1)
    acts_pair = pair_order(h == 0, acts_mine, swap(acts_sent, "yl")).reshape(2 * own_tokens, -1)
    acts_all = lax.all_gather(acts_pair, "z", axis=0, tiled=True)

    w_mine = lax.dynamic_slice_in_dim(weight[0], h * half, half, 0)
    w_sent = lax.dynamic_slice_in_dim(weight[0], (1 - h) * half, half, 0)
    w_pair = jnp.concatenate([w_mine, swap(w_sent, "yl")], axis=1)
    w_all = lax.all_gather(w_pair, "x", axis=0, tiled=True)

    g_half = lax.dynamic_slice_in_dim(out_grad, c * (tokens // 2), tokens // 2, 0)
    g_got = y_ring(g_half)
    g_other = pair_order(c == 0, g_got, swap(g_got, "c")).reshape(tokens, width)
    g_pair = jnp.concatenate([out_grad, g_other], axis=1)

    partial = dot(g_pair, w_all, ((1,), (1,)))
    summed = lax.psum_scatter(partial, "z", scatter_dimension=0, tiled=True).astype(BF16)
    s_mine = lax.dynamic_slice_in_dim(summed, h * own_tokens, own_tokens, 0)
    s_sent = lax.dynamic_slice_in_dim(summed, (1 - h) * own_tokens, own_tokens, 0)
    s_pair = pair_order(h == 0, s_mine, swap(s_sent, "yl"))
    input_grad = s_pair.reshape(2, own_tokens, owners, half).transpose(1, 2, 0, 3)

    folded = dot(acts_all, g_pair, ((0,), (0,)))
    owned = lax.psum_scatter(folded, "x", scatter_dimension=0, tiled=True)
    weight_grad = pair_order(h == 0, owned[:, :width], swap(owned[:, width:], "yl"))
    return input_grad.reshape(own_tokens, features), weight_grad.reshape(1, rows, width)


def solution(mesh):
    dp, out, in_ = mesh.devices.shape
    fine = Mesh(mesh.devices.reshape(dp, out // 2, 2, 2, in_ // 2), ("x", "z", "yl", "yh", "c"))
    tokens, split = P(("x", "z", "yl"), ("yh", "c")), P(("yh", "c"), "x", ("z", "yl"))
    return jax.shard_map(
        on_device,
        mesh=fine,
        in_specs=(tokens, P("x", ("z", "yl")), split),
        out_specs=(tokens, split),
        check_vma=False,
    )
```

time: 659 us -> 295 us (0.45)
  waiting for transfers between devices: 619 us -> 236 us
  local copies, waits for them, and re-layouts: 0.01 us -> 10.6 us
  starting transfers between devices: 0.16 us -> 8.38 us
    reduce_scatter x2, waiting for transfers between devices: 402 us -> 146 us  [the longest x1 95.8 us: on_device(): lax.psum_scatter(partial, 'z', scatter_dimension=0, tiled=True).astype(BF16)]
    all_gather x2, waiting for transfers between devices: 215 us -> 58.2 us  [the longest x1 30.8 us: on_device(): acts_all = lax.all_gather(acts_pair, 'z', axis=0, tiled=True)]
    ppermute x0 -> x6, waiting for transfers between devices: none -> 31.9 us  [the longest x5 21.8 us: swap(): return lax.ppermute(a, axis, [(0, 1), (1, 0)])]
    ppermute x0 -> x6, starting transfers between devices: none -> 8.04 us  [the longest x5 7.51 us: swap(): return lax.ppermute(a, axis, [(0, 1), (1, 0)])]
  transfers between devices with their start and end apart: 4 -> 10, of which waited for: 4 -> 9; matrix products, arithmetic and copies ran while one was open for 4% -> 9% of each run, Pallas kernels for 0% -> 0%
where the time goes in v1:
time: 295 us; the launch traced here: 294 us
  waiting for transfers between devices  236 us (80%)
  matrix products  19.9 us (7%)
  between operations  13.9 us (5%)
  local copies, waits for them, and re-layouts  10.6 us (4%)
  starting transfers between devices  8.38 us (3%)
  other arithmetic  5.29 us (2%)
    reduce_scatter x1, waiting for transfers between devices, on_device(): lax.psum_scatter(partial, 'z', scatter_dimension=0, tiled=True).astype(BF16)  95.8 us
    reduce_scatter x1, waiting for transfers between devices, on_device(): owned = lax.psum_scatter(folded, 'x', scatter_dimension=0, tiled=True)  50.2 us
    all_gather x1, waiting for transfers between devices, on_device(): acts_all = lax.all_gather(acts_pair, 'z', axis=0, tiled=True)  30.8 us
    all_gather x1, waiting for transfers between devices, on_device(): w_all = lax.all_gather(w_pair, 'x', axis=0, tiled=True)  27.4 us
    ppermute x5, waiting for transfers between devices, swap(): return lax.ppermute(a, axis, [(0, 1), (1, 0)])  21.8 us
    dot_general x2, matrix products, dot(): return lax.dot_general(a, b, (dims, ((), ())), preferred_element_type=F32)  19.9 us
    ppermute x1, waiting for transfers between devices, y_ring(): return lax.ppermute(a, ('yl', 'yh', 'c'), perm)  10.1 us
    ppermute x5, starting transfers between devices, swap(): return lax.ppermute(a, axis, [(0, 1), (1, 0)])  7.51 us
  transfers between devices with their start and end apart: 10, of which 9 were waited for; matrix products, arithmetic and copies ran while one was open for 9% of the time, Pallas kernels for 0%

profile of v1, /device:TPU:4, one launch (start us, length us, event | category | flops | bytes accessed | tf_op | source)
XLA Modules:
  0.0 294.4 jit_solution(6356978120530604813)
XLA Ops:
  7.2 0.0 all-gather.5.cloned.1.call-start
  7.2 1.4 reshape.36
  8.6 0.0 copy-start.1
  8.7 3.3 %dynamic-slice_reduce_fusion.1 = (bf16[128,4,256]{2,1,0:T(4,128)(2,1)S(1)}, bf16[128,4,256]{2,1,0:T(4,128)(2,1)S(1)}) fusion(bf16[128,4,2,256]{3,2,1,0:T(2,128)(2,1)S(1)} %reshape.36, s32[]{:T(128)S(6)} %select_n.78, s32[]{:T(128)S(6)} %select_n.79), kind=kLoop, calls=%fused_computation.13 | loop fusion | bytes 1048584 | tf_op jit(solution)/shard_map/jit(dynamic_index_in_dim)/dynamic_slice | solution.py:41
  12.0 1.7 collective-permute-start.4
  13.7 6.4 %collective-permute-done.4 = bf16[128,1024]{1,0:T(8,128)(2,1)S(1)} collective-permute-done((bf16[128,1024]{1,0:T(8,128)(2,1)S(1)}, bf16[128,1024]{1,0:T(8,128)(2,1)S(1)}, u32[]{:S(2)}, u32[]{:S(2)}) %collective-permute-start.4) | collective-permute-done | bytes 262176 | tf_op jit(solution)/shard_map/ppermute | solution.py:15
  20.2 0.8 pad_maximum_fusion.6
  21.0 0.0 all-gather.5.cloned.1.call-update
  21.0 0.0 all-gather.3.cloned.1.call-start
  21.1 0.0 copy-done.1
  21.1 0.8 dynamic-slice_bitcast_fusion.1
  21.9 1.6 collective-permute-start.2
  23.5 1.4 constant_dynamic-slice_fusion.1
  24.9 0.5 collective-permute-start
  25.4 7.3 %collective-permute-done.2 = bf16[256,640]{1,0:T(8,128)(2,1)S(1)} collective-permute-done((bf16[256,640]{1,0:T(8,128)(2,1)}, bf16[256,640]{1,0:T(8,128)(2,1)S(1)}, u32[]{:S(2)}, u32[]{:S(2)}) %collective-permute-start.2) | collective-permute-done | bytes 327712 | tf_op jit(solution)/shard_map/ppermute | solution.py:15
  32.8 0.9 pad_maximum_fusion.5
  33.6 0.0 all-gather.3.cloned.1.call-update
  33.7 0.0 reduce-scatter.5.cloned.1.call-start
  33.7 10.1 %collective-permute-done = bf16[1024,640]{1,0:T(8,128)(2,1)S(1)} collective-permute-done((bf16[1024,640]{1,0:T(8,128)(2,1)S(1)}, bf16[1024,640]{1,0:T(8,128)(2,1)S(1)}, u32[]{:S(2)}, u32[]{:S(2)}) %collective-permute-start) | collective-permute-done | bytes 1310752 | tf_op jit(solution)/shard_map/ppermute | solution.py:24
  43.8 1.1 collective-permute-start.1
  45.0 2.7 collective-permute-done.1
  47.6 0.2 select_bitcast_fusion.1
  47.9 0.3 pad_maximum_fusion.3
  48.1 30.8 %all-gather.5.cloned.1.call-done = bf16[2048,1024]{1,0:T(8,128)(2,1)} async-done(((bf16[256,1024]{1,0:T(8,128)(2,1)}), bf16[2048,1024]{1,0:T(8,128)(2,1)}) %all-gather.5.cloned.1.call-update) | async-done | bytes 4194320 | tf_op jit(solution)/shard_map/all_gather | solution.py:44
  78.9 9.9 %fusion = f32[1024,1280]{1,0:T(8,128)} fusion(bf16[2048,1024]{1,0:T(8,128)(2,1)} %all-gather.5.cloned.1.call-done, bf16[2048,640]{1,0:T(8,128)(2,1)S(1)} %bitcast.27, bf16[2048,640]{1,0:T(8,128)(2,1)} %param.4), kind=kOutput, calls=%fused_computation.1 | convolution fusion | flops 5379194880 | bytes 14680064 | tf_op jit(solution)/shard_map/dot_general | solution.py:28
  88.8 0.0 reduce-scatter.5.cloned.1.call-update
  88.9 0.2 reduce-scatter.3.cloned.1.call-start
  89.1 27.4 %all-gather.3.cloned.1.call-done = bf16[1024,1280]{1,0:T(8,128)(2,1)} async-done(((bf16[256,1280]{1,0:T(8,128)(2,1)}), bf16[1024,1280]{1,0:T(8,128)(2,1)}) %all-gather.3.cloned.1.call-update) | async-done | bytes 2621456 | tf_op jit(solution)/shard_map/all_gather | solution.py:49
  116.5 10.0 %fusion.1 = f32[2048,1024]{1,0:T(8,128)} fusion(bf16[1024,1280]{1,0:T(8,128)(2,1)} %all-gather.3.cloned.1.call-done, bf16[2048,640]{1,0:T(8,128)(2,1)S(1)} %bitcast.28, bf16[2048,640]{1,0:T(8,128)(2,1)} %param.4), kind=kOutput, calls=%fused_computation.2 | convolution fusion | flops 5379194880 | bytes 16252928 | tf_op jit(solution)/shard_map/dot_general | solution.py:28
  126.6 0.0 reduce-scatter.3.cloned.1.call-update
  126.6 50.2 %reduce-scatter.5.cloned.1.call-done = f32[256,1280]{1,0:T(8,128)} async-done(((f32[1024,1280]{1,0:T(8,128)}), f32[256,1280]{1,0:T(8,128)}) %reduce-scatter.5.cloned.1.call-update) | async-done | bytes 1310736 | tf_op jit(solution)/shard_map/reduce_scatter | solution.py:64
  176.8 0.0 copy-start
  176.8 1.2 slice.9
  178.1 1.6 collective-permute-start.5
  179.6 95.8 %reduce-scatter.3.cloned.1.call-done = f32[256,1024]{1,0:T(8,128)} async-done(((f32[2048,1024]{1,0:T(8,128)}), f32[256,1024]{1,0:T(8,128)}) %reduce-scatter.3.cloned.1.call-update) | async-done | bytes 1048592 | tf_op jit(solution)/shard_map/reduce_scatter | solution.py:57
  275.4 1.3 convert_element_type.3
  276.8 1.6 collective-permute-start.3
  278.4 0.0 collective-permute-done.5
  278.4 0.0 copy-done
  278.4 0.1 select_bitcast_fusion.3
  278.4 1.1 pad_maximum_fusion.4
  279.6 5.4 %collective-permute-done.3 = bf16[128,1024]{1,0:T(8,128)(2,1)S(1)} collective-permute-done((bf16[128,1024]{1,0:T(8,128)(2,1)S(1)}, bf16[128,1024]{1,0:T(8,128)(2,1)S(1)}, u32[]{:S(2)}, u32[]{:S(2)}) %collective-permute-start.3) | collective-permute-done | bytes 262176 | tf_op jit(solution)/shard_map/ppermute | solution.py:15
  285.0 0.1 broadcast_select_fusion.1
  285.1 0.2 stack.40
  285.3 0.2 stack.39
  285.5 0.4 maximum_bitcast_fusion
  285.8 0.8 copy.5
  286.7 1.2 reshape.35
  (4 shorter events, 0.1 us)
Async XLA Ops:
  7.2 71.8 %all-gather.5.cloned.1.call-start = ((), (), s32[]{:S(2)}) async-start(), calls=%async_computation.4 | async-start | bytes 4718592 | tf_op jit(solution)/shard_map/all_gather | solution.py:44
  8.6 12.5 %copy-start.1 = (bf16[1,512,640]{2,1,0:T(8,128)(2,1)S(1)}, bf16[1,512,640]{2,1,0:T(8,128)(2,1)}, u32[]{:S(2)}) copy-start(bf16[1,512,640]{2,1,0:T(8,128)(2,1)} %param.5) | copy-start | bytes 1966084
  12.0 8.1 %collective-permute-start.4 = (bf16[128,1024]{1,0:T(8,128)(2,1)S(1)}, bf16[128,1024]{1,0:T(8,128)(2,1)S(1)}, u32[]{:S(2)}, u32[]{:S(2)}) collective-permute-start(bf16[128,1024]{1,0:T(8,128)(2,1)S(1)} %bitcast.34), channel_id=1, source_target_pairs={{0,4},{4,0},{1,5},{5,1},{2,6},{6,2},{3,7},{7,3},{8,12},{12,8},{9,1... | collective-permute-start | bytes 786440 | tf_op jit(solution)/shard_map/ppermute | solution.py:15
  21.0 95.5 %all-gather.3.cloned.1.call-start = ((), (), s32[]{:S(2)}) async-start(), calls=%async_computation.2 | async-start | bytes 3276800 | tf_op jit(solution)/shard_map/all_gather | solution.py:49
  21.9 10.9 %collective-permute-start.2 = (bf16[256,640]{1,0:T(8,128)(2,1)}, bf16[256,640]{1,0:T(8,128)(2,1)S(1)}, u32[]{:S(2)}, u32[]{:S(2)}) collective-permute-start(bf16[256,640]{1,0:T(8,128)(2,1)} %get-tuple-element.11), channel_id=1, source_target_pairs={{0,4},{4,0},{1,5},{5,1},{2,6},{6,2},{3,7},{7,3},{8,12},{12,8},{9,1... | collective-permute-start | bytes 983048 | tf_op jit(solution)/shard_map/ppermute | solution.py:15
  24.9 18.9 %collective-permute-start = (bf16[1024,640]{1,0:T(8,128)(2,1)S(1)}, bf16[1024,640]{1,0:T(8,128)(2,1)S(1)}, u32[]{:S(2)}, u32[]{:S(2)}) collective-permute-start(bf16[1024,640]{1,0:T(8,128)(2,1)S(1)} %constant_dynamic-slice_fusion.1), channel_id=1, source_target_pairs={{0,4},{1,7},{4,2},{5,1},{2,6},{3,5},{6,0},{7,3},{8,12},{9,15},{12,... | collective-permute-start | bytes 3932168 | tf_op jit(solution)/shard_map/ppermute | solution.py:24
  33.7 143.2 %reduce-scatter.5.cloned.1.call-start = ((), (), s32[]{:S(2)}) async-start(), calls=%async_computation.5 | async-start | bytes 6553600 | tf_op jit(solution)/shard_map/reduce_scatter | solution.py:64
  43.8 3.8 %collective-permute-start.1 = (bf16[1024,640]{1,0:T(8,128)(2,1)S(1)}, bf16[1024,640]{1,0:T(8,128)(2,1)S(1)}, u32[]{:S(2)}, u32[]{:S(2)}) collective-permute-start(bf16[1024,640]{1,0:T(8,128)(2,1)S(1)} %collective-permute-done), channel_id=1, source_target_pairs={{0,1},{1,0},{2,3},{3,2},{4,5},{5,4},{6,7},{7,6},{8,9},{9,8},{10,11... | collective-permute-start | bytes 3932168 | tf_op jit(solution)/shard_map/ppermute | solution.py:15
  88.9 186.6 %reduce-scatter.3.cloned.1.call-start = ((), (), s32[]{:S(2)}) async-start(), calls=%async_computation.3 | async-start | bytes 9437184 | tf_op jit(solution)/shard_map/reduce_scatter | solution.py:57
  176.8 101.5 %copy-start = (f32[256,1280]{1,0:T(8,128)S(1)}, f32[256,1280]{1,0:T(8,128)}, u32[]{:S(2)}) copy-start(f32[256,1280]{1,0:T(8,128)} %reduce-scatter.5.cloned.1.call-done) | copy-start | bytes 3932164
  178.1 100.3 %collective-permute-start.5 = (f32[256,640]{1,0:T(8,128)S(1)}, f32[256,640]{1,0:T(8,128)S(1)}, u32[]{:S(2)}, u32[]{:S(2)}) collective-permute-start(f32[256,640]{1,0:T(8,128)S(1)} %slice.9), channel_id=1, source_target_pairs={{0,4},{4,0},{1,5},{5,1},{2,6},{6,2},{3,7},{7,3},{8,12},{12,8},{9,1... | collective-permute-start | bytes 1966088 | tf_op jit(solution)/shard_map/ppermute | solution.py:15
  276.8 8.2 %collective-permute-start.3 = (bf16[128,1024]{1,0:T(8,128)(2,1)S(1)}, bf16[128,1024]{1,0:T(8,128)(2,1)S(1)}, u32[]{:S(2)}, u32[]{:S(2)}) collective-permute-start(bf16[128,1024]{1,0:T(8,128)(2,1)S(1)} %constant_dynamic-slice_fusion), channel_id=1, source_target_pairs={{0,4},{4,0},{1,5},{5,1},{2,6},{6,2},{3,7},{7,3},{8,12},{12,8},{9,1... | collective-permute-start | bytes 786440 | tf_op jit(solution)/shard_map/ppermute | solution.py:15
Sparse Core Ops, SparseCore 0:
  21.2 57.7 all-gather.4
  81.3 35.1 all-gather.2
  119.1 57.6 reduce-scatter.4
  179.2 96.1 reduce-scatter.2

commit v2 on v1

v2 whole, which is shorter than its diff:
```python
import functools

import jax
import jax.numpy as jnp
from jax import lax
from jax.experimental import pallas as pl
from jax.experimental.pallas import tpu as pltpu
from jax.sharding import Mesh, PartitionSpec as P

F32 = jnp.float32
BF16 = jnp.bfloat16
LANES = 128
TILE = 16
SQUARINGS = 4
TOP = 2.0**7.75
TINY = 1e-30


def encode(v, s):
    a = jnp.abs(v) * s
    for _ in range(SQUARINGS):
        a = a * a
    return jnp.where(v < 0, -a, a).astype(BF16)


def decode(y, inv):
    y = y.astype(F32)
    a = jnp.abs(y)
    for _ in range(SQUARINGS):
        a = jnp.sqrt(a)
    a = a * inv
    return jnp.where(y < 0, -a, a)


def inverse_scale(ref):
    return 1.0 / ref[ref.shape[0] - TILE :, :].astype(F32)


def for_tiles(rows, body, init):
    return lax.fori_loop(0, rows // TILE, lambda i, x: body(pl.multiple_of(i * TILE, TILE), x), init)


def write_coded(v_ref, first, blocks, amax, out_ref):
    rows = v_ref.shape[0]
    top = jnp.max(jnp.max(amax, axis=1, keepdims=True), axis=0, keepdims=True)
    coded = jnp.broadcast_to(TOP / jnp.maximum(top, TINY), (TILE, LANES)).astype(BF16)
    s = coded.astype(F32)
    out_ref[blocks * rows :, :] = coded

    def body(r, x):
        for j in range(blocks):
            at = (first + j) * LANES
            out_ref[pl.ds(j * rows + r, TILE), :] = encode(v_ref[pl.ds(r, TILE), at : at + LANES], s)
        return x

    for_tiles(rows, body, 0)


def summed_tile(own_ref, got, invs, r, j):
    rows = own_ref.shape[0]
    v = own_ref[pl.ds(r, TILE), j * LANES : (j + 1) * LANES]
    for ref, inv in zip(got, invs):
        v = v + decode(ref[pl.ds(j * rows + r, TILE), :], inv)
    return v


def hop_kernel(n_got, idx_ref, *refs):
    got, own_ref, out_ref, v_ref = refs[:n_got], refs[n_got], refs[n_got + 1], refs[n_got + 2]
    blocks = own_ref.shape[1] // LANES
    invs = [inverse_scale(ref) for ref in got]

    def body(r, amax):
        for j in range(blocks):
            v = summed_tile(own_ref, got, invs, r, j)
            v_ref[pl.ds(r, TILE), j * LANES : (j + 1) * LANES] = v
            amax = jnp.maximum(amax, jnp.abs(v))
        return amax

    amax = for_tiles(own_ref.shape[0], body, jnp.zeros((TILE, LANES), F32))
    write_coded(v_ref, 0, blocks, amax, out_ref)


def tokens_kernel(idx_ref, f_ref, b_ref, own_ref, out_ref):
    invs = [inverse_scale(f_ref), inverse_scale(b_ref)]

    def body(r, x):
        for j in range(own_ref.shape[1] // LANES):
            v = summed_tile(own_ref, (f_ref, b_ref), invs, r, j)
            out_ref[pl.ds(r, TILE), j * LANES : (j + 1) * LANES] = v.astype(BF16)
        return x

    for_tiles(own_ref.shape[0], body, 0)


def owned_kernel(idx_ref, f_ref, b_ref, own_ref, mine_ref, out_ref, v_ref):
    invs = [inverse_scale(f_ref), inverse_scale(b_ref)]
    blocks = own_ref.shape[1] // LANES
    kept = blocks // 2

    def body(r, amax):
        for j in range(blocks):
            v = summed_tile(own_ref, (f_ref, b_ref), invs, r, j)
            if j < kept:
                mine_ref[pl.ds(r, TILE), j * LANES : (j + 1) * LANES] = v
            else:
                v_ref[pl.ds(r, TILE), (j - kept) * LANES : (j - kept + 1) * LANES] = v
                amax = jnp.maximum(amax, jnp.abs(v))
        return amax

    amax = for_tiles(own_ref.shape[0], body, jnp.zeros((TILE, LANES), F32))
    write_coded(v_ref, 0, blocks - kept, amax, out_ref)


def rows_kernel(h_ref, mine_ref, got_ref, out_ref):
    rows = mine_ref.shape[0]
    inv = inverse_scale(got_ref)
    mine_at, got_at = h_ref[0] * rows, (1 - h_ref[0]) * rows

    def body(r, x):
        out_ref[pl.ds(pl.multiple_of(mine_at + r, TILE), TILE), :] = mine_ref[pl.ds(r, TILE), :]
        for j in range(mine_ref.shape[1] // LANES):
            v = decode(got_ref[pl.ds(j * rows + r, TILE), :], inv)
            out_ref[pl.ds(pl.multiple_of(got_at + r, TILE), TILE), j * LANES : (j + 1) * LANES] = v
        return x

    for_tiles(rows, body, 0)


def whole(shape):
    return pl.BlockSpec(shape, lambda i, idx: (0,) * len(shape))


def call(kernel, idx, got, own, out_shapes, scratch=()):
    in_specs, args = [whole(a.shape) for a in got], list(got)
    if own is not None:
        in_specs.append(pl.BlockSpec((own[1], own[0].shape[1]), lambda i, idx: (idx[0], 0)))
        args.append(own[0])
    size = sum(a.size * 4 for a in got) + sum(s.size * 4 for s in out_shapes)
    return pl.pallas_call(
        kernel,
        grid_spec=pltpu.PrefetchScalarGridSpec(
            num_scalar_prefetch=1,
            grid=(1,),
            in_specs=in_specs,
            out_specs=[whole(s.shape) for s in out_shapes],
            scratch_shapes=[pltpu.VMEM(s, F32) for s in scratch],
        ),
        out_shape=out_shapes,
        compiler_params=pltpu.CompilerParams(vmem_limit_bytes=24 * 1024 * 1024),
        cost_estimate=pl.CostEstimate(flops=size * 8, bytes_accessed=size, transcendentals=0),
    )(jnp.reshape(idx, (1,)).astype(jnp.int32), *args)


def coded_shape(rows, width):
    return jax.ShapeDtypeStruct((width // LANES * rows + TILE, LANES), BF16)


def hop(got, total, rows, idx):
    width = total.shape[1]
    kernel = functools.partial(hop_kernel, len(got))
    return call(kernel, idx, got, (total, rows), [coded_shape(rows, width)], [(rows, width)])[0]


def swap(a, axis):
    return lax.ppermute(a, axis, [(0, 1), (1, 0)])


def y_ring(a):
    perm = []
    for y in range(4):
        for c in range(2):
            t = (y + (1 if c == 0 else -1)) % 4
            perm.append((((y % 2) * 2 + y // 2) * 2 + c, ((t % 2) * 2 + t // 2) * 2 + c))
    return lax.ppermute(a, ("yl", "yh", "c"), perm)


def ring(a, axis, way):
    n = lax.axis_size(axis)
    perm = [(i * 2 + c, (i + (way if c == 0 else -way)) % n * 2 + c) for i in range(n) for c in range(2)]
    return lax.ppermute(a, (axis, "c"), perm)


def gathered(a, axis, step):
    n, me = lax.axis_size(axis), lax.axis_index(axis)
    blocks = {0: a}
    ahead = back = a
    for k in range(1, n // 2 + 1):
        ahead = blocks[-k] = ring(ahead, axis, 1)
        if k < n - n // 2:
            back = blocks[k] = ring(back, axis, -1)
    buf = jnp.zeros((n,) + a.shape, a.dtype)
    for k, b in blocks.items():
        buf = lax.dynamic_update_index_in_dim(buf, b, lax.rem(me + step * k + n, n), 0)
    return buf.reshape((-1,) + a.shape[1:])


def scattered(total, axis, step):
    n, me = lax.axis_size(axis), lax.axis_index(axis)
    rows = total.shape[0] // n
    ahead, back = [], []
    for k in range(n // 2, 0, -1):
        ahead = [ring(hop(ahead, total, rows, lax.rem(me + step * k + n, n)), axis, 1)]
        if k < n - n // 2:
            back = [ring(hop(back, total, rows, lax.rem(me - step * k + n, n)), axis, -1)]
    return ahead + back


def dot(a, b, dims):
    return lax.dot_general(a, b, (dims, ((), ())), preferred_element_type=F32)


def interleaved(first, mine, other, width):
    parts = []
    for j in range(0, mine.shape[1], width):
        m, o = mine[:, j : j + width], other[:, j : j + width]
        parts += [jnp.where(first, m, o), jnp.where(first, o, m)]
    return jnp.concatenate(parts, axis=1)


def on_device(activations, out_grad, weight):
    h = lax.axis_index("yl")
    c = lax.axis_index("c")
    step = 1 - 2 * c
    tokens, width = out_grad.shape
    own_tokens, features = activations.shape
    rows = weight.shape[1]
    half = rows // 2
    owners = features // rows

    low = jnp.concatenate([activations[:, d * rows : d * rows + half] for d in range(owners)], axis=1)
    high = jnp.concatenate([activations[:, d * rows + half : (d + 1) * rows] for d in range(owners)], axis=1)
    acts_mine, acts_sent = jnp.where(h == 0, low, high), jnp.where(h == 0, high, low)
    acts_got = swap(acts_sent, "yl")
    acts_pair = jnp.concatenate([jnp.where(h == 0, acts_mine, acts_got), jnp.where(h == 0, acts_got, acts_mine)])
    acts_all = gathered(acts_pair, "z", step)

    w_mine = jnp.where(h == 0, weight[0, :half], weight[0, half:])
    w_sent = jnp.where(h == 0, weight[0, half:], weight[0, :half])
    w_pair = jnp.concatenate([w_mine, swap(w_sent, "yl")], axis=1)
    w_all = gathered(w_pair, "x", step)

    g_got = y_ring(jnp.where(c == 0, out_grad[: tokens // 2], out_grad[tokens // 2 :]))
    g_rest = swap(g_got, "c")
    g_other = jnp.concatenate([jnp.where(c == 0, g_got, g_rest), jnp.where(c == 0, g_rest, g_got)])
    g_pair = jnp.concatenate([out_grad, g_other], axis=1)

    partial = dot(g_pair, w_all, ((1,), (1,)))
    shape = jax.ShapeDtypeStruct((2 * own_tokens, features // 2), BF16)
    came = scattered(partial, "z", step)
    summed = call(tokens_kernel, lax.axis_index("z"), came, (partial, 2 * own_tokens), [shape])[0]
    s_mine = jnp.where(h == 0, summed[:own_tokens], summed[own_tokens:])
    s_sent = jnp.where(h == 0, summed[own_tokens:], summed[:own_tokens])
    input_grad = interleaved(h == 0, s_mine, swap(s_sent, "yl"), half)

    folded = dot(acts_all, g_pair, ((0,), (0,)))
    came = scattered(folded, "x", step)
    shapes = [jax.ShapeDtypeStruct((half, width), F32), coded_shape(half, width)]
    owned, coded = call(owned_kernel, lax.axis_index("x"), came, (folded, half), shapes, [(half, width)])
    shape = jax.ShapeDtypeStruct((rows, width), F32)
    weight_grad = call(rows_kernel, h, (owned, swap(coded, "yl")), None, [shape])[0]
    return input_grad, weight_grad[None]


def solution(mesh):
    dp, out, in_ = mesh.devices.shape
    fine = Mesh(mesh.devices.reshape(dp, out // 2, 2, 2, in_ // 2), ("x", "z", "yl", "yh", "c"))
    tokens, split = P(("x", "z", "yl"), ("yh", "c")), P(("yh", "c"), "x", ("z", "yl"))
    return jax.shard_map(
        on_device,
        mesh=fine,
        in_specs=(tokens, P("x", ("z", "yl")), split),
        out_specs=(tokens, split),
        check_vma=False,
    )
```

time: 295 us -> 159 us (0.54)
  waiting for transfers between devices: 236 us -> 57.9 us
  Pallas kernels: 0 us -> 29.8 us
  starting transfers between devices: 8.38 us -> 33.7 us
  between operations: 13.9 us -> 1.13 us
  matrix products: 19.9 us -> 11.8 us
  local copies, waits for them, and re-layouts: 10.6 us -> 16 us
    reduce_scatter x2 -> x0, waiting for transfers between devices: 146 us -> none  [the longest x1 95.8 us: on_device(): lax.psum_scatter(partial, 'z', scatter_dimension=0, tiled=True).astype(BF16)]
    all_gather x2 -> x0, waiting for transfers between devices: 58.2 us -> none  [the longest x1 30.8 us: on_device(): acts_all = lax.all_gather(acts_pair, 'z', axis=0, tiled=True)]
    ppermute x0 -> x20, waiting for transfers between devices: none -> 47.7 us  [ring(): return lax.ppermute(a, (axis, 'c'), perm)]
    pallas_call x0 -> x13, Pallas kernels: none -> 29.8 us  [call(): pl.pallas_call(kernel, grid_spec=pltpu.PrefetchScalarGridSpec(num_scalar_...]
    ppermute x0 -> x20, starting transfers between devices: none -> 26.3 us  [ring(): return lax.ppermute(a, (axis, 'c'), perm)]
    unnamed x6 -> x26, local copies, waits for them, and re-layouts: 0.07 us -> 13.1 us
    ppermute x5, waiting for transfers between devices: 21.8 us -> 10.3 us  [swap(): return lax.ppermute(a, axis, [(0, 1), (1, 0)])]
    ppermute x1, waiting for transfers between devices: 10.1 us -> 0.01 us  [y_ring(): return lax.ppermute(a, ('yl', 'yh', 'c'), perm)]
  transfers between devices with their start and end apart: 10 -> 26, of which waited for: 9 -> 8; matrix products, arithmetic and copies ran while one was open for 9% -> 13% of each run, Pallas kernels for 0% -> 19%
where the time goes in v2:
time: 159 us; the launch traced here: 158 us
  waiting for transfers between devices  57.9 us (36%)
  starting transfers between devices  33.7 us (21%)
  Pallas kernels  29.8 us (19%)
  local copies, waits for them, and re-layouts  16 us (10%)
  matrix products  11.8 us (7%)
  other arithmetic  8.03 us (5%)
    ppermute x20, waiting for transfers between devices, ring(): return lax.ppermute(a, (axis, 'c'), perm)  47.7 us
    pallas_call x13, Pallas kernels, call(): pl.pallas_call(kernel, grid_spec=pltpu.PrefetchScalarGridSpec(num_scalar_...  29.8 us
    ppermute x20, starting transfers between devices, ring(): return lax.ppermute(a, (axis, 'c'), perm)  26.3 us
    unnamed x26, local copies, waits for them, and re-layouts  13.1 us
    dot_general x2, matrix products, dot(): return lax.dot_general(a, b, (dims, ((), ())), preferred_element_type=F32)  11.8 us
    ppermute x5, waiting for transfers between devices, swap(): return lax.ppermute(a, axis, [(0, 1), (1, 0)])  10.3 us
    ppermute x5, starting transfers between devices, swap(): return lax.ppermute(a, axis, [(0, 1), (1, 0)])  5.76 us
  transfers between devices with their start and end apart: 26, of which 8 were waited for; matrix products, arithmetic and copies ran while one was open for 13% of the time, Pallas kernels for 19%

profile of v2, /device:TPU:4, one launch (start us, length us, event | category | flops | bytes accessed | tf_op | source)
XLA Modules:
  0.0 158.3 jit_solution(7626537336418490019)
XLA Ops:
  0.6 2.0 %select_bitcast_fusion.1 = (bf16[256,640]{1,0:T(8,128)(2,1)S(1)}, bf16[256,640]{1,0:T(8,128)(2,1)}) fusion(pred[]{:T(512)S(6)} %eq.4, bf16[1,512,640]{2,1,0:T(8,128)(2,1)} %param.5), kind=kLoop, calls=%fused_computation.21 | loop fusion | flops 327680 | bytes 1310721 | tf_op jit(solution)/shard_map/jit(_where)/select_n | solution.py:237
  2.7 1.6 collective-permute-start.2
  4.2 1.8 %fusion.4 = (bf16[128,256]{1,0:T(8,128)(2,1)S(1)}, bf16[128,256]{1,0:T(8,128)(2,1)S(1)}, bf16[128,256]{1,0:T(8,128)(2,1)S(1)}, bf16[128,256]{1,0:T(8,128)(2,1)S(...) fusion(bf16[128,2048]{1,0:T(8,128)(2,1)} %param.3), kind=kLoop, calls=%fused_computation.40 | loop fusion | bytes 1048576 | tf_op jit(solution)/shard_map/slice | solution.py:230
  6.6 1.7 %broadcast_select_fusion.4 = bf16[128,1024]{1,0:T(8,128)(2,1)} fusion(pred[]{:T(512)S(6)} %eq.4, bf16[128,256]{1,0:T(8,128)(2,1)} %get-tuple-element.18, bf16[128,256]{1,0:T(8,128)(2,1)S(1)} %get-tuple-element.19, bf16[128,256]{1,0:T(8,128)(2,1)S(1)} %get-tuple-element.13, bf16[128,256]{1,0:T(8,128)(2,1)S(1)} %get-tuple-element.14, ...), kind=kLoop, calls=%fused_computation.26 | loop fusion | flops 2228224 | bytes 786433 | tf_op jit(solution)/shard_map/jit(_where)/select_n | solution.py:232
  8.8 1.2 slice_select_fusion
  10.0 1.6 collective-permute-start
  11.5 7.7 %collective-permute-done.14 = bf16[128,1024]{1,0:T(8,128)(2,1)} collective-permute-done((bf16[128,1024]{1,0:T(8,128)(2,1)}, bf16[128,1024]{1,0:T(8,128)(2,1)}, u32[]{:S(2)}, u32[]{:S(2)}) %collective-permute-start.14) | collective-permute-done | bytes 262176 | tf_op jit(solution)/shard_map/ppermute | solution.py:165
  19.2 1.1 broadcast_select_fusion.3
  20.4 2.0 %collective-permute-start.15 = (bf16[256,1024]{1,0:T(8,128)(2,1)S(1)}, bf16[256,1024]{1,0:T(8,128)(2,1)S(1)}, u32[]{:S(2)}, u32[]{:S(2)}) collective-permute-start(bf16[256,1024]{1,0:T(8,128)(2,1)S(1)} %pad_maximum_fusion.1), channel_id=1, source_target_pairs={{0,8},{1,57},{8,16},{9,1},{16,24},{17,9},{24,32},{25,17},{32,40},{... | collective-permute-start | bytes 1572872 | tf_op jit(solution)/shard_map/ppermute | solution.py:180
  22.4 4.0 %collective-permute-start.16 = (bf16[256,1024]{1,0:T(8,128)(2,1)S(1)}, bf16[256,1024]{1,0:T(8,128)(2,1)S(1)}, u32[]{:S(2)}, u32[]{:S(2)}) collective-permute-start(bf16[256,1024]{1,0:T(8,128)(2,1)S(1)} %pad_maximum_fusion.1), channel_id=1, source_target_pairs={{0,56},{1,9},{8,0},{9,17},{16,8},{17,25},{24,16},{25,33},{32,24},{... | collective-permute-start | bytes 1572872 | tf_op jit(solution)/shard_map/ppermute | solution.py:180
  27.1 1.3 collective-permute-start.3
  28.3 0.8 collective-permute-start.4
  29.4 9.5 %collective-permute-done.15 = bf16[256,1024]{1,0:T(8,128)(2,1)S(1)} collective-permute-done((bf16[256,1024]{1,0:T(8,128)(2,1)S(1)}, bf16[256,1024]{1,0:T(8,128)(2,1)S(1)}, u32[]{:S(2)}, u32[]{:S(2)}) %collective-permute-start.15) | collective-permute-done | bytes 524320 | tf_op jit(solution)/shard_map/ppermute | solution.py:180
  38.9 3.2 %collective-permute-start.18 = (bf16[256,1024]{1,0:T(8,128)(2,1)S(1)}, bf16[256,1024]{1,0:T(8,128)(2,1)S(1)}, u32[]{:S(2)}, u32[]{:S(2)}) collective-permute-start(bf16[256,1024]{1,0:T(8,128)(2,1)S(1)} %collective-permute-done.16), channel_id=1, source_target_pairs={{0,56},{1,9},{8,0},{9,17},{16,8},{17,25},{24,16},{25,33},{32,24},{... | collective-permute-start | bytes 1572872 | tf_op jit(solution)/shard_map/ppermute | solution.py:180
  42.2 1.3 collective-permute-start.5
  43.7 10.1 %collective-permute-done.17 = bf16[256,1024]{1,0:T(8,128)(2,1)S(1)} collective-permute-done((bf16[256,1024]{1,0:T(8,128)(2,1)S(1)}, bf16[256,1024]{1,0:T(8,128)(2,1)S(1)}, u32[]{:S(2)}, u32[]{:S(2)}) %collective-permute-start.17) | collective-permute-done | bytes 524320 | tf_op jit(solution)/shard_map/ppermute | solution.py:180
  53.8 3.2 %collective-permute-start.20 = (bf16[256,1024]{1,0:T(8,128)(2,1)S(1)}, bf16[256,1024]{1,0:T(8,128)(2,1)S(1)}, u32[]{:S(2)}, u32[]{:S(2)}) collective-permute-start(bf16[256,1024]{1,0:T(8,128)(2,1)S(1)} %collective-permute-done.18), channel_id=1, source_target_pairs={{0,56},{1,9},{8,0},{9,17},{16,8},{17,25},{24,16},{25,33},{32,24},{... | collective-permute-start | bytes 1572872 | tf_op jit(solution)/shard_map/ppermute | solution.py:180
  57.2 10.7 %collective-permute-done.19 = bf16[256,1024]{1,0:T(8,128)(2,1)S(1)} collective-permute-done((bf16[256,1024]{1,0:T(8,128)(2,1)S(1)}, bf16[256,1024]{1,0:T(8,128)(2,1)S(1)}, u32[]{:S(2)}, u32[]{:S(2)}) %collective-permute-start.19) | collective-permute-done | bytes 524320 | tf_op jit(solution)/shard_map/ppermute | solution.py:180
  67.9 1.6 %broadcast_select_fusion.1 = (bf16[1024,640]{1,0:T(8,128)(2,1)S(1)}, bf16[1024,640]{1,0:T(8,128)(2,1)S(1)}) fusion(bf16[1024,640]{1,0:T(8,128)(2,1)} %collective-permute-done, bf16[1024,640]{1,0:T(8,128)(2,1)S(1)} %collective-permute-done.1, pred[]{:T(512)S(6)} %eq.5), kind=kLoop, calls=%fused_computation.5 | loop fusion | flops 1310720 | bytes 5242881 | tf_op jit(solution)/shard_map/jit(_where)/select_n | solution.py:244
  69.5 5.7 %fusion.1.refs_0_.refs_1_.own_ref = f32[2048,1024]{1,0:T(8,128)S(1)} fusion(bf16[1024,1280]{1,0:T(8,128)(2,1)S(1)} %bitcast.51, bf16[1024,640]{1,0:T(8,128)(2,1)S(1)} %get-tuple-element.7, bf16[1024,640]{1,0:T(8,128)(2,1)S(1)} %get-tuple-element.6, bf16[2048,640]{1,0:T(8,128)(2,1)S(1)} %copy-done.5), kind=kOutput, calls=%fused_computation.2 | convolution fusion | flops 5384437760 | bytes 16252928 | tf_op jit(solution)/shard_map/dot_general | solution.py:209
  76.2 5.6 %collective-permute-done.21 = bf16[256,1024]{1,0:T(8,128)(2,1)S(1)} collective-permute-done((bf16[256,1024]{1,0:T(8,128)(2,1)S(1)}, bf16[256,1024]{1,0:T(8,128)(2,1)S(1)}, u32[]{:S(2)}, u32[]{:S(2)}) %collective-permute-start.21) | collective-permute-done | bytes 524320 | tf_op jit(solution)/shard_map/ppermute | solution.py:180
  82.7 6.9 %collective-permute-done.6.refs_0_ = bf16[2064,128]{1,0:T(8,128)(2,1)S(1)} collective-permute-done((bf16[2064,128]{1,0:T(8,128)(2,1)S(1)}, bf16[2064,128]{1,0:T(8,128)(2,1)S(1)}, u32[]{:S(2)}, u32[]{:S(2)}) %collective-permute-start.6) | collective-permute-done | bytes 528416 | tf_op jit(solution)/shard_map/ppermute | solution.py:180
  89.7 2.1 %shard_map.51 = bf16[2064,128]{1,0:T(8,128)(2,1)S(1)} custom-call(s32[1]{0:T(128)} %bitcast.3.idx_ref, bf16[2064,128]{1,0:T(8,128)(2,1)S(1)} %collective-permute-done.6.refs_0_, f32[2048,1024]{1,0:T(8,128)S(1)} %fusion.1.refs_0_.refs_1_.own_ref), custom_call_target="tpu_custom_call" | custom-call | flops 16908288 | bytes 2113536 | tf_op jit(solution)/shard_map/pallas_call | solution.py:139
  92.1 6.1 %fusion.refs_0_.refs_1_.own_ref = f32[1024,1280]{1,0:T(8,128)S(1)} fusion(bf16[2048,1024]{1,0:T(8,128)(2,1)S(1)} %bitcast.50, bf16[1024,640]{1,0:T(8,128)(2,1)S(1)} %get-tuple-element.7, bf16[1024,640]{1,0:T(8,128)(2,1)S(1)} %get-tuple-element.6, bf16[2048,640]{1,0:T(8,128)(2,1)S(1)} %copy-done.6), kind=kOutput, calls=%fused_computation.1 | convolution fusion | flops 5384437760 | bytes 14680064 | tf_op jit(solution)/shard_map/dot_general | solution.py:209
  98.2 0.9 shard_map.58
  99.1 2.4 %copy-done.3 = f32[1024,1280]{1,0:T(8,128)} copy-done((f32[1024,1280]{1,0:T(8,128)}, f32[1024,1280]{1,0:T(8,128)S(1)}, u32[]{:S(2)}) %copy-start.3) | copy-done | bytes 5242904
  101.5 1.2 collective-permute-start.22
  102.7 3.4 %copy-done.1 = f32[2048,1024]{1,0:T(8,128)S(1)} copy-done((f32[2048,1024]{1,0:T(8,128)S(1)}, f32[2048,1024]{1,0:T(8,128)}, u32[]{:S(2)}) %copy-start.1) | copy-done | bytes 8388632
  106.0 3.1 %shard_map.55 = bf16[2064,128]{1,0:T(8,128)(2,1)S(1)} custom-call(s32[1]{0:T(128)} %bitcast.13.idx_ref, bf16[2064,128]{1,0:T(8,128)(2,1)} %collective-permute-done.10.refs_0_, f32[2048,1024]{1,0:T(8,128)S(1)} %copy-done.1), custom_call_target="tpu_custom_call" | custom-call | flops 16908288 | bytes 2113536 | tf_op jit(solution)/shard_map/pallas_call | solution.py:139
  109.2 3.3 %collective-permute-start.11 = (bf16[2064,128]{1,0:T(8,128)(2,1)S(1)}, bf16[2064,128]{1,0:T(8,128)(2,1)}, u32[]{:S(2)}, u32[]{:S(2)}) collective-permute-start(bf16[2064,128]{1,0:T(8,128)(2,1)S(1)} %shard_map.55), channel_id=1, source_target_pairs={{0,56},{1,9},{8,0},{9,17},{16,8},{17,25},{24,16},{25,33},{32,24},{... | collective-permute-start | bytes 1585160 | tf_op jit(solution)/shard_map/ppermute | solution.py:180
  112.5 2.9 %shard_map.52 = bf16[2064,128]{1,0:T(8,128)(2,1)} custom-call(s32[1]{0:T(128)} %bitcast.2.idx_ref, bf16[2064,128]{1,0:T(8,128)(2,1)S(1)} %collective-permute-done.7.refs_0_, f32[2048,1024]{1,0:T(8,128)S(1)} %copy-done.1), custom_call_target="tpu_custom_call" | custom-call | flops 16908288 | bytes 2113536 | tf_op jit(solution)/shard_map/pallas_call | solution.py:139
  115.4 2.5 %copy-done.4 = f32[1024,1280]{1,0:T(8,128)S(1)} copy-done((f32[1024,1280]{1,0:T(8,128)S(1)}, f32[1024,1280]{1,0:T(8,128)}, u32[]{:S(2)}) %copy-start.4) | copy-done | bytes 5242904
  117.8 0.8 shard_map.60
  118.7 0.9 collective-permute-start.24
  119.6 3.4 %shard_map.59 = bf16[2576,128]{1,0:T(8,128)(2,1)} custom-call(s32[1]{0:T(128)} %bitcast.17.idx_ref, bf16[2576,128]{1,0:T(8,128)(2,1)S(1)} %collective-permute-done.22.refs_0_, f32[1024,1280]{1,0:T(8,128)S(1)} %copy-done.4), custom_call_target="tpu_custom_call" | custom-call | flops 21102592 | bytes 2637824 | tf_op jit(solution)/shard_map/pallas_call | solution.py:139
  123.0 1.2 collective-permute-start.23
  124.2 3.4 %copy-done.2 = f32[2048,1024]{1,0:T(8,128)S(1)} copy-done((f32[2048,1024]{1,0:T(8,128)S(1)}, f32[2048,1024]{1,0:T(8,128)}, u32[]{:S(2)}) %copy-start.2) | copy-done | bytes 8388632
  127.6 3.3 %shard_map.56 = bf16[2064,128]{1,0:T(8,128)(2,1)S(1)} custom-call(s32[1]{0:T(128)} %bitcast.12.idx_ref, bf16[2064,128]{1,0:T(8,128)(2,1)} %collective-permute-done.11.refs_0_, f32[2048,1024]{1,0:T(8,128)S(1)} %copy-done.2), custom_call_target="tpu_custom_call" | custom-call | flops 16908288 | bytes 2113536 | tf_op jit(solution)/shard_map/pallas_call | solution.py:139
  130.9 3.3 %collective-permute-start.12 = (bf16[2064,128]{1,0:T(8,128)(2,1)S(1)}, bf16[2064,128]{1,0:T(8,128)(2,1)S(1)}, u32[]{:S(2)}, u32[]{:S(2)}) collective-permute-start(bf16[2064,128]{1,0:T(8,128)(2,1)S(1)} %shard_map.56), channel_id=1, source_target_pairs={{0,56},{1,9},{8,0},{9,17},{16,8},{17,25},{24,16},{25,33},{32,24},{... | collective-permute-start | bytes 1585160 | tf_op jit(solution)/shard_map/ppermute | solution.py:180
  134.2 3.3 %shard_map.53 = bf16[2064,128]{1,0:T(8,128)(2,1)S(1)} custom-call(s32[1]{0:T(128)} %bitcast.1.idx_ref, bf16[2064,128]{1,0:T(8,128)(2,1)} %collective-permute-done.8.refs_0_, f32[2048,1024]{1,0:T(8,128)S(1)} %copy-done.2), custom_call_target="tpu_custom_call" | custom-call | flops 16908288 | bytes 2113536 | tf_op jit(solution)/shard_map/pallas_call | solution.py:139
  137.6 3.7 %shard_map.61 = (f32[256,640]{1,0:T(8,128)S(1)}, bf16[1296,128]{1,0:T(8,128)(2,1)S(1)}) custom-call(s32[1]{0:T(128)} %bitcast.16.idx_ref, bf16[2576,128]{1,0:T(8,128)(2,1)S(1)} %collective-permute-done.23.f_ref, bf16[2576,128]{1,0:T(8,128)(2,1)S(1)} %collective-permute-done.24.b_ref, f32[1024,1280]{1,0:T(8,128)S(1)} %bitcast.49), custom_call_target="tpu_custom_call" | custom-call | flops 31653888 | bytes 3956736 | tf_op jit(solution)/shard_map/pallas_call | solution.py:139
  141.3 1.8 %collective-permute-start.25 = (bf16[1296,128]{1,0:T(8,128)(2,1)S(1)}, bf16[1296,128]{1,0:T(8,128)(2,1)S(1)}, u32[]{:S(2)}, u32[]{:S(2)}) collective-permute-start(bf16[1296,128]{1,0:T(8,128)(2,1)S(1)} %get-tuple-element.5), channel_id=1, source_target_pairs={{0,4},{4,0},{1,5},{5,1},{2,6},{6,2},{3,7},{7,3},{8,12},{12,8},{9,1... | collective-permute-start | bytes 995336 | tf_op jit(solution)/shard_map/ppermute | solution.py:165
  143.2 4.8 %collective-permute-done.9.f_ref = bf16[2064,128]{1,0:T(8,128)(2,1)S(1)} collective-permute-done((bf16[2064,128]{1,0:T(8,128)(2,1)S(1)}, bf16[2064,128]{1,0:T(8,128)(2,1)S(1)}, u32[]{:S(2)}, u32[]{:S(2)}) %collective-permute-start.9) | collective-permute-done | bytes 528416 | tf_op jit(solution)/shard_map/ppermute | solution.py:180
  148.0 2.8 %shard_map.57 = bf16[256,1024]{1,0:T(8,128)(2,1)S(1)} custom-call(s32[1]{0:T(128)} %bitcast.idx_ref, bf16[2064,128]{1,0:T(8,128)(2,1)S(1)} %collective-permute-done.9.f_ref, bf16[2064,128]{1,0:T(8,128)(2,1)S(1)} %collective-permute-done.12.b_ref, f32[2048,1024]{1,0:T(8,128)S(1)} %bitcast.47), custom_call_target="tpu_custom_call" | custom-call | flops 25296896 | bytes 3162112 | tf_op jit(solution)/shard_map/pallas_call | solution.py:139
  150.8 1.8 %collective-permute-start.13 = (bf16[128,1024]{1,0:T(8,128)(2,1)S(1)}, bf16[128,1024]{1,0:T(8,128)(2,1)S(1)}, u32[]{:S(2)}, u32[]{:S(2)}) collective-permute-start(bf16[128,1024]{1,0:T(8,128)(2,1)S(1)} %get-tuple-element.21), channel_id=1, source_target_pairs={{0,4},{4,0},{1,5},{5,1},{2,6},{6,2},{3,7},{7,3},{8,12},{12,8},{9,1... | collective-permute-start | bytes 786440 | tf_op jit(solution)/shard_map/ppermute | solution.py:165
  152.6 2.0 %shard_map.62 = f32[512,640]{1,0:T(8,128)} custom-call(s32[1]{0:T(128)} %bitcast.15.h_ref, f32[256,640]{1,0:T(8,128)S(1)} %get-tuple-element.4.mine_ref, bf16[1296,128]{1,0:T(8,128)(2,1)S(1)} %collective-permute-done.25.got_ref), custom_call_target="tpu_custom_call" | custom-call | flops 21037056 | bytes 2629632 | tf_op jit(solution)/shard_map/pallas_call | solution.py:139
  154.7 2.6 %collective-permute-done.13 = bf16[128,1024]{1,0:T(8,128)(2,1)S(1)} collective-permute-done((bf16[128,1024]{1,0:T(8,128)(2,1)S(1)}, bf16[128,1024]{1,0:T(8,128)(2,1)S(1)}, u32[]{:S(2)}, u32[]{:S(2)}) %collective-permute-start.13) | collective-permute-done | bytes 262176 | tf_op jit(solution)/shard_map/ppermute | solution.py:165
  157.5 0.8 copy-done.8
  (78 shorter events, 4.8 us)
Async XLA Ops:
  0.6 8.1 %copy-start.5 = (bf16[2048,640]{1,0:T(8,128)(2,1)S(1)}, bf16[2048,640]{1,0:T(8,128)(2,1)}, u32[]{:S(2)}) copy-start(bf16[2048,640]{1,0:T(8,128)(2,1)} %param.4) | copy-start | bytes 7864324
  2.7 24.3 %collective-permute-start.2 = (bf16[256,640]{1,0:T(8,128)(2,1)}, bf16[256,640]{1,0:T(8,128)(2,1)S(1)}, u32[]{:S(2)}, u32[]{:S(2)}) collective-permute-start(bf16[256,640]{1,0:T(8,128)(2,1)} %get-tuple-element.11), channel_id=1, source_target_pairs={{0,4},{4,0},{1,5},{5,1},{2,6},{6,2},{3,7},{7,3},{8,12},{12,8},{9,1... | collective-permute-start | bytes 983048 | tf_op jit(solution)/shard_map/ppermute | solution.py:165
  6.0 0.6 copy-start.7
  8.3 10.9 %collective-permute-start.14 = (bf16[128,1024]{1,0:T(8,128)(2,1)}, bf16[128,1024]{1,0:T(8,128)(2,1)}, u32[]{:S(2)}, u32[]{:S(2)}) collective-permute-start(bf16[128,1024]{1,0:T(8,128)(2,1)} %broadcast_select_fusion.4), channel_id=1, source_target_pairs={{0,4},{4,0},{1,5},{5,1},{2,6},{6,2},{3,7},{7,3},{8,12},{12,8},{9,1... | collective-permute-start | bytes 786440 | tf_op jit(solution)/shard_map/ppermute | solution.py:165
  10.0 33.6 %collective-permute-start = (bf16[1024,640]{1,0:T(8,128)(2,1)}, bf16[1024,640]{1,0:T(8,128)(2,1)}, u32[]{:S(2)}, u32[]{:S(2)}) collective-permute-start(bf16[1024,640]{1,0:T(8,128)(2,1)} %slice_select_fusion), channel_id=1, source_target_pairs={{0,4},{1,7},{4,2},{5,1},{2,6},{3,5},{6,0},{7,3},{8,12},{9,15},{12,... | collective-permute-start | bytes 3932168 | tf_op jit(solution)/shard_map/ppermute | solution.py:174
  20.4 18.5 %collective-permute-start.15 = (bf16[256,1024]{1,0:T(8,128)(2,1)S(1)}, bf16[256,1024]{1,0:T(8,128)(2,1)S(1)}, u32[]{:S(2)}, u32[]{:S(2)}) collective-permute-start(bf16[256,1024]{1,0:T(8,128)(2,1)S(1)} %pad_maximum_fusion.1), channel_id=1, source_target_pairs={{0,8},{1,57},{8,16},{9,1},{16,24},{17,9},{24,32},{25,17},{32,40},{... | collective-permute-start | bytes 1572872 | tf_op jit(solution)/shard_map/ppermute | solution.py:180
  22.4 16.5 %collective-permute-start.16 = (bf16[256,1024]{1,0:T(8,128)(2,1)S(1)}, bf16[256,1024]{1,0:T(8,128)(2,1)S(1)}, u32[]{:S(2)}, u32[]{:S(2)}) collective-permute-start(bf16[256,1024]{1,0:T(8,128)(2,1)S(1)} %pad_maximum_fusion.1), channel_id=1, source_target_pairs={{0,56},{1,9},{8,0},{9,17},{16,8},{17,25},{24,16},{25,33},{32,24},{... | collective-permute-start | bytes 1572872 | tf_op jit(solution)/shard_map/ppermute | solution.py:180
  27.1 15.2 %collective-permute-start.3 = (bf16[256,1280]{1,0:T(8,128)(2,1)S(1)}, bf16[256,1280]{1,0:T(8,128)(2,1)S(1)}, u32[]{:S(2)}, u32[]{:S(2)}) collective-permute-start(bf16[256,1280]{1,0:T(8,128)(2,1)S(1)} %pad_maximum_fusion), channel_id=1, source_target_pairs={{0,64},{1,193},{64,128},{65,1},{128,192},{129,65},{192,0},{193,129... | collective-permute-start | bytes 1966088 | tf_op jit(solution)/shard_map/ppermute | solution.py:180
  28.3 15.3 %collective-permute-start.4 = (bf16[256,1280]{1,0:T(8,128)(2,1)S(1)}, bf16[256,1280]{1,0:T(8,128)(2,1)S(1)}, u32[]{:S(2)}, u32[]{:S(2)}) collective-permute-start(bf16[256,1280]{1,0:T(8,128)(2,1)S(1)} %pad_maximum_fusion), channel_id=1, source_target_pairs={{0,192},{1,65},{64,0},{65,129},{128,64},{129,193},{192,128},{193,1... | collective-permute-start | bytes 1966088 | tf_op jit(solution)/shard_map/ppermute | solution.py:180
  38.9 15.0 %collective-permute-start.17 = (bf16[256,1024]{1,0:T(8,128)(2,1)S(1)}, bf16[256,1024]{1,0:T(8,128)(2,1)S(1)}, u32[]{:S(2)}, u32[]{:S(2)}) collective-permute-start(bf16[256,1024]{1,0:T(8,128)(2,1)S(1)} %collective-permute-done.15), channel_id=1, source_target_pairs={{0,8},{1,57},{8,16},{9,1},{16,24},{17,9},{24,32},{25,17},{32,40},{... | collective-permute-start | bytes 1572872 | tf_op jit(solution)/shard_map/ppermute | solution.py:180
  38.9 15.0 %collective-permute-start.18 = (bf16[256,1024]{1,0:T(8,128)(2,1)S(1)}, bf16[256,1024]{1,0:T(8,128)(2,1)S(1)}, u32[]{:S(2)}, u32[]{:S(2)}) collective-permute-start(bf16[256,1024]{1,0:T(8,128)(2,1)S(1)} %collective-permute-done.16), channel_id=1, source_target_pairs={{0,56},{1,9},{8,0},{9,17},{16,8},{17,25},{24,16},{25,33},{32,24},{... | collective-permute-start | bytes 1572872 | tf_op jit(solution)/shard_map/ppermute | solution.py:180
  42.2 14.9 %collective-permute-start.5 = (bf16[256,1280]{1,0:T(8,128)(2,1)S(1)}, bf16[256,1280]{1,0:T(8,128)(2,1)S(1)}, u32[]{:S(2)}, u32[]{:S(2)}) collective-permute-start(bf16[256,1280]{1,0:T(8,128)(2,1)S(1)} %collective-permute-done.3), channel_id=1, source_target_pairs={{0,64},{1,193},{64,128},{65,1},{128,192},{129,65},{192,0},{193,129... | collective-permute-start | bytes 1966088 | tf_op jit(solution)/shard_map/ppermute | solution.py:180
  43.6 24.4 %collective-permute-start.1 = (bf16[1024,640]{1,0:T(8,128)(2,1)}, bf16[1024,640]{1,0:T(8,128)(2,1)S(1)}, u32[]{:S(2)}, u32[]{:S(2)}) collective-permute-start(bf16[1024,640]{1,0:T(8,128)(2,1)} %collective-permute-done), channel_id=1, source_target_pairs={{0,1},{1,0},{2,3},{3,2},{4,5},{5,4},{6,7},{7,6},{8,9},{9,8},{10,11... | collective-permute-start | bytes 3932168 | tf_op jit(solution)/shard_map/ppermute | solution.py:165
  53.8 14.1 %collective-permute-start.19 = (bf16[256,1024]{1,0:T(8,128)(2,1)S(1)}, bf16[256,1024]{1,0:T(8,128)(2,1)S(1)}, u32[]{:S(2)}, u32[]{:S(2)}) collective-permute-start(bf16[256,1024]{1,0:T(8,128)(2,1)S(1)} %collective-permute-done.17), channel_id=1, source_target_pairs={{0,8},{1,57},{8,16},{9,1},{16,24},{17,9},{24,32},{25,17},{32,40},{... | collective-permute-start | bytes 1572872 | tf_op jit(solution)/shard_map/ppermute | solution.py:180
  53.8 22.3 %collective-permute-start.20 = (bf16[256,1024]{1,0:T(8,128)(2,1)S(1)}, bf16[256,1024]{1,0:T(8,128)(2,1)S(1)}, u32[]{:S(2)}, u32[]{:S(2)}) collective-permute-start(bf16[256,1024]{1,0:T(8,128)(2,1)S(1)} %collective-permute-done.18), channel_id=1, source_target_pairs={{0,56},{1,9},{8,0},{9,17},{16,8},{17,25},{24,16},{25,33},{32,24},{... | collective-permute-start | bytes 1572872 | tf_op jit(solution)/shard_map/ppermute | solution.py:180
  67.9 13.9 %collective-permute-start.21 = (bf16[256,1024]{1,0:T(8,128)(2,1)S(1)}, bf16[256,1024]{1,0:T(8,128)(2,1)S(1)}, u32[]{:S(2)}, u32[]{:S(2)}) collective-permute-start(bf16[256,1024]{1,0:T(8,128)(2,1)S(1)} %collective-permute-done.19), channel_id=1, source_target_pairs={{0,8},{1,57},{8,16},{9,1},{16,24},{17,9},{24,32},{25,17},{32,40},{... | collective-permute-start | bytes 1572872 | tf_op jit(solution)/shard_map/ppermute | solution.py:180
  75.3 14.4 %copy-start = (f32[2048,1024]{1,0:T(8,128)}, f32[2048,1024]{1,0:T(8,128)S(1)}, u32[]{:S(2)}) copy-start(f32[2048,1024]{1,0:T(8,128)S(1)} %fusion.1.refs_0_.refs_1_.own_ref) | copy-start | bytes 25165828
  76.0 13.6 %collective-permute-start.6 = (bf16[2064,128]{1,0:T(8,128)(2,1)S(1)}, bf16[2064,128]{1,0:T(8,128)(2,1)S(1)}, u32[]{:S(2)}, u32[]{:S(2)}) collective-permute-start(bf16[2064,128]{1,0:T(8,128)(2,1)S(1)} %shard_map.50), channel_id=1, source_target_pairs={{0,8},{1,57},{8,16},{9,1},{16,24},{17,9},{24,32},{25,17},{32,40},{... | collective-permute-start | bytes 1585160 | tf_op jit(solution)/shard_map/ppermute | solution.py:180
  82.6 20.0 %collective-permute-start.10 = (bf16[2064,128]{1,0:T(8,128)(2,1)S(1)}, bf16[2064,128]{1,0:T(8,128)(2,1)}, u32[]{:S(2)}, u32[]{:S(2)}) collective-permute-start(bf16[2064,128]{1,0:T(8,128)(2,1)S(1)} %shard_map.54), channel_id=1, source_target_pairs={{0,56},{1,9},{8,0},{9,17},{16,8},{17,25},{24,16},{25,33},{32,24},{... | collective-permute-start | bytes 1585160 | tf_op jit(solution)/shard_map/ppermute | solution.py:180
  89.7 2.4 %copy-start.6 = (bf16[2048,640]{1,0:T(8,128)(2,1)S(1)}, bf16[2048,640]{1,0:T(8,128)(2,1)}, u32[]{:S(2)}) copy-start(bf16[2048,640]{1,0:T(8,128)(2,1)} %param.4) | copy-start | bytes 7864324
  91.7 20.7 %collective-permute-start.7 = (bf16[2064,128]{1,0:T(8,128)(2,1)S(1)}, bf16[2064,128]{1,0:T(8,128)(2,1)S(1)}, u32[]{:S(2)}, u32[]{:S(2)}) collective-permute-start(bf16[2064,128]{1,0:T(8,128)(2,1)S(1)} %shard_map.51), channel_id=1, source_target_pairs={{0,8},{1,57},{8,16},{9,1},{16,24},{17,9},{24,32},{25,17},{32,40},{... | collective-permute-start | bytes 1585160 | tf_op jit(solution)/shard_map/ppermute | solution.py:180
  99.1 2.4 %copy-start.3 = (f32[1024,1280]{1,0:T(8,128)}, f32[1024,1280]{1,0:T(8,128)S(1)}, u32[]{:S(2)}) copy-start(f32[1024,1280]{1,0:T(8,128)S(1)} %fusion.refs_0_.refs_1_.own_ref) | copy-start | bytes 15728644
  101.5 18.2 %collective-permute-start.22 = (bf16[2576,128]{1,0:T(8,128)(2,1)S(1)}, bf16[2576,128]{1,0:T(8,128)(2,1)S(1)}, u32[]{:S(2)}, u32[]{:S(2)}) collective-permute-start(bf16[2576,128]{1,0:T(8,128)(2,1)S(1)} %shard_map.58), channel_id=1, source_target_pairs={{0,64},{1,193},{64,128},{65,1},{128,192},{129,65},{192,0},{193,129... | collective-permute-start | bytes 1978376 | tf_op jit(solution)/shard_map/ppermute | solution.py:180
  102.7 3.4 %copy-start.1 = (f32[2048,1024]{1,0:T(8,128)S(1)}, f32[2048,1024]{1,0:T(8,128)}, u32[]{:S(2)}) copy-start(f32[2048,1024]{1,0:T(8,128)} %copy-done) | copy-start | bytes 25165828
  109.2 15.0 %collective-permute-start.11 = (bf16[2064,128]{1,0:T(8,128)(2,1)S(1)}, bf16[2064,128]{1,0:T(8,128)(2,1)}, u32[]{:S(2)}, u32[]{:S(2)}) collective-permute-start(bf16[2064,128]{1,0:T(8,128)(2,1)S(1)} %shard_map.55), channel_id=1, source_target_pairs={{0,56},{1,9},{8,0},{9,17},{16,8},{17,25},{24,16},{25,33},{32,24},{... | collective-permute-start | bytes 1585160 | tf_op jit(solution)/shard_map/ppermute | solution.py:180
  115.4 18.8 %collective-permute-start.8 = (bf16[2064,128]{1,0:T(8,128)(2,1)}, bf16[2064,128]{1,0:T(8,128)(2,1)}, u32[]{:S(2)}, u32[]{:S(2)}) collective-permute-start(bf16[2064,128]{1,0:T(8,128)(2,1)} %shard_map.52), channel_id=1, source_target_pairs={{0,8},{1,57},{8,16},{9,1},{16,24},{17,9},{24,32},{25,17},{32,40},{... | collective-permute-start | bytes 1585160 | tf_op jit(solution)/shard_map/ppermute | solution.py:180
  115.4 2.5 %copy-start.4 = (f32[1024,1280]{1,0:T(8,128)S(1)}, f32[1024,1280]{1,0:T(8,128)}, u32[]{:S(2)}) copy-start(f32[1024,1280]{1,0:T(8,128)} %copy-done.3) | copy-start | bytes 15728644
  118.7 18.9 %collective-permute-start.24 = (bf16[2576,128]{1,0:T(8,128)(2,1)S(1)}, bf16[2576,128]{1,0:T(8,128)(2,1)S(1)}, u32[]{:S(2)}, u32[]{:S(2)}) collective-permute-start(bf16[2576,128]{1,0:T(8,128)(2,1)S(1)} %shard_map.60), channel_id=1, source_target_pairs={{0,192},{1,65},{64,0},{65,129},{128,64},{129,193},{192,128},{193,1... | collective-permute-start | bytes 1978376 | tf_op jit(solution)/shard_map/ppermute | solution.py:180
  119.6 18.0 %slice-start.2 = ((s8[5242880]{0:T(1024)(128)(4,1)}), s8[1048576]{0:T(1024)(128)(4,1)S(1)}, s32[]{:S(2)}) async-start(s8[5242880]{0:T(1024)(128)(4,1)} %bitcast.48), calls=%async_computation.2 | async-start | bytes 2097152
  123.0 14.6 %collective-permute-start.23 = (bf16[2576,128]{1,0:T(8,128)(2,1)}, bf16[2576,128]{1,0:T(8,128)(2,1)S(1)}, u32[]{:S(2)}, u32[]{:S(2)}) collective-permute-start(bf16[2576,128]{1,0:T(8,128)(2,1)} %shard_map.59), channel_id=1, source_target_pairs={{0,64},{1,193},{64,128},{65,1},{128,192},{129,65},{192,0},{193,129... | collective-permute-start | bytes 1978376 | tf_op jit(solution)/shard_map/ppermute | solution.py:180
  124.2 3.4 %copy-start.2 = (f32[2048,1024]{1,0:T(8,128)S(1)}, f32[2048,1024]{1,0:T(8,128)}, u32[]{:S(2)}) copy-start(f32[2048,1024]{1,0:T(8,128)} %copy-done) | copy-start | bytes 25165828
  127.6 10.0 %slice-start.3 = ((s8[5242880]{0:T(1024)(128)(4,1)}), s8[4194304]{0:T(1024)(128)(4,1)S(1)}, s32[]{:S(2)}) async-start(s8[5242880]{0:T(1024)(128)(4,1)} %bitcast.48), calls=%async_computation.3 | async-start | bytes 8388608
  130.9 12.3 %collective-permute-start.12 = (bf16[2064,128]{1,0:T(8,128)(2,1)S(1)}, bf16[2064,128]{1,0:T(8,128)(2,1)S(1)}, u32[]{:S(2)}, u32[]{:S(2)}) collective-permute-start(bf16[2064,128]{1,0:T(8,128)(2,1)S(1)} %shard_map.56), channel_id=1, source_target_pairs={{0,56},{1,9},{8,0},{9,17},{16,8},{17,25},{24,16},{25,33},{32,24},{... | collective-permute-start | bytes 1585160 | tf_op jit(solution)/shard_map/ppermute | solution.py:180
  134.2 13.8 %slice-start = ((s8[8388608]{0:T(1024)(128)(4,1)}), s8[4194304]{0:T(1024)(128)(4,1)S(1)}, s32[]{:S(2)}) async-start(s8[8388608]{0:T(1024)(128)(4,1)} %bitcast.46), calls=%async_computation | async-start | bytes 8388608
  134.2 13.8 %slice-start.1 = ((s8[8388608]{0:T(1024)(128)(4,1)}), s8[4194304]{0:T(1024)(128)(4,1)S(1)}, s32[]{:S(2)}) async-start(s8[8388608]{0:T(1024)(128)(4,1)} %bitcast.46), calls=%async_computation.1 | async-start | bytes 8388608
  137.5 10.5 %collective-permute-start.9 = (bf16[2064,128]{1,0:T(8,128)(2,1)S(1)}, bf16[2064,128]{1,0:T(8,128)(2,1)S(1)}, u32[]{:S(2)}, u32[]{:S(2)}) collective-permute-start(bf16[2064,128]{1,0:T(8,128)(2,1)S(1)} %shard_map.53), channel_id=1, source_target_pairs={{0,8},{1,57},{8,16},{9,1},{16,24},{17,9},{24,32},{25,17},{32,40},{... | collective-permute-start | bytes 1585160 | tf_op jit(solution)/shard_map/ppermute | solution.py:180
  141.3 11.3 %collective-permute-start.25 = (bf16[1296,128]{1,0:T(8,128)(2,1)S(1)}, bf16[1296,128]{1,0:T(8,128)(2,1)S(1)}, u32[]{:S(2)}, u32[]{:S(2)}) collective-permute-start(bf16[1296,128]{1,0:T(8,128)(2,1)S(1)} %get-tuple-element.5), channel_id=1, source_target_pairs={{0,4},{4,0},{1,5},{5,1},{2,6},{6,2},{3,7},{7,3},{8,12},{12,8},{9,1... | collective-permute-start | bytes 995336 | tf_op jit(solution)/shard_map/ppermute | solution.py:165
  150.8 6.5 %collective-permute-start.13 = (bf16[128,1024]{1,0:T(8,128)(2,1)S(1)}, bf16[128,1024]{1,0:T(8,128)(2,1)S(1)}, u32[]{:S(2)}, u32[]{:S(2)}) collective-permute-start(bf16[128,1024]{1,0:T(8,128)(2,1)S(1)} %get-tuple-element.21), channel_id=1, source_target_pairs={{0,4},{4,0},{1,5},{5,1},{2,6},{6,2},{3,7},{7,3},{8,12},{12,8},{9,1... | collective-permute-start | bytes 786440 | tf_op jit(solution)/shard_map/ppermute | solution.py:165
  157.5 0.8 copy-start.8
